TPU v7x, 32 devices: a whole 2x2x4 slice. The times are simulated.
32 devices in a mesh: groups: 2 (over y), ep: 4 (over x, core), tp: 4 (over z).
Axes of the slice: x: 2, y: 2, z: 4, core: 2. Of those that a mesh axis runs over, the one named last changes fastest.
Arguments:
- x_moe: bfloat16 [512, 7168], P(('groups', 'ep'), 'tp'), parts along dimension 0, may hold values from -6 to 6
- routes: int32 [512, 2], P(('groups', 'ep')), parts along dimension 0, may hold values from 0 to 3, all different within a row; in each aligned block of 64 rows (0 to 63, 64 to 127, ...) at most 48 rows name the same one
- router_logits: float32 [512, 2], P(('groups', 'ep')), parts along dimension 0, may hold values from -6 to 6
- w_gate: bfloat16 [4, 7168, 2048], P('ep', None, 'tp'), may hold values from -0.0625 to 0.0625
- w_up: bfloat16 [4, 7168, 2048], P('ep', None, 'tp'), may hold values from -0.0625 to 0.0625
- w_down: bfloat16 [4, 2048, 7168], P('ep', 'tp'), may hold values from -0.125 to 0.125
- q_latent: bfloat16 [512, 64, 512], P(('groups', 'ep'), 'tp'), parts along dimension 0, may hold values from -96 to 96
- q_rope: bfloat16 [512, 4096], P(('groups', 'ep'), 'tp'), parts along dimension 0, may hold values from -96 to 96
- kv_latent: bfloat16 [512, 512], P(('groups', 'ep')), parts along dimension 0, may hold values from -6 to 6
- key_rope: bfloat16 [512, 64], P(('groups', 'ep')), parts along dimension 0, may hold values from -6 to 6
- prompt_lengths: int32 [16], P('groups'), parts along dimension 0, may hold values from 1 to 128, 256 in all
Outputs:
- moe_out: bfloat16 [512, 7168], P(('groups', 'ep'), 'tp'), parts along dimension 0
- context: bfloat16 [512, 64, 512], P(('groups', 'ep'), 'tp'), parts along dimension 0
There are 2 independent parts, one for each index of `groups`. A program takes and returns all parts, laid end to end along the dimension named above; an argument that names none is the same for every part. Nothing has to cross between parts.
Inputs may be any that keep to these rules, and one draw needn't show every extreme that they name: `routes`: in each aligned block of 64 rows (the rows of one device) no expert is named by more than 48 rows, a bound that some block reaches; every expert is named somewhere; the 2 experts of a row differ. `prompt_lengths`: the lengths sum to 256; the largest is exactly 128.
All inputs are finite; a program needn't handle non-finite values.
Results may differ from a plain program's by a relative error of at most 0.011.
Values may be sent and summed in bfloat16 or wider, within the bound.
A program may use at most 128 MiB of HBM per device.

v0:
```python
import jax
import jax.numpy as jnp
from jax import lax
from jax.sharding import PartitionSpec as P

CAP = 48


score_scale = 192.0 ** (-0.5)
route_scale = 2.5


def prompt_of(lengths, positions):
    ends = jnp.cumsum(lengths)
    return jnp.sum((positions[:, None] >= ends[None, :]).astype(jnp.int32), axis=1)


def attend(q_latent, q_rope, kv_latent, key_rope, prompt_lengths):
    rows, heads, width = q_latent.shape
    rope = key_rope.shape[1]
    q_pos = lax.axis_index("ep") * rows + jnp.arange(rows, dtype=jnp.int32)
    q_prompt = prompt_of(prompt_lengths, q_pos)
    flat_lat = q_latent.reshape(rows * heads, width)
    flat_rot = q_rope.reshape(rows * heads, rope)
    row_pos = jnp.repeat(q_pos, heads)
    row_prompt = jnp.repeat(q_prompt, heads)
    top = jnp.full((rows * heads,), -1e30, jnp.float32)
    keys = lax.all_gather(kv_latent, "ep", axis=0, tiled=True)
    rot_keys = lax.all_gather(key_rope, "ep", axis=0, tiled=True)
    k_pos = jnp.arange(keys.shape[0], dtype=jnp.int32)
    k_prompt = prompt_of(prompt_lengths, k_pos)
    visible = (row_prompt[:, None] == k_prompt[None, :]) & (k_pos[None, :] <= row_pos[:, None])
    scores = (
        jnp.einsum("rd,kd->rk", flat_lat, keys, preferred_element_type=jnp.float32)
        + jnp.einsum("rd,kd->rk", flat_rot, rot_keys, preferred_element_type=jnp.float32)
    ) * score_scale
    masked = jnp.where(visible, scores, -1e30)
    new_top = jnp.maximum(top, jnp.max(masked, axis=1))
    weights = jnp.where(visible, jnp.exp(masked - new_top[:, None]), 0.0)
    total = jnp.sum(weights, axis=1)
    accum = jnp.dot(weights.astype(jnp.bfloat16), keys, preferred_element_type=jnp.float32)
    top, total, accum = (new_top, total, accum)
    return (accum / total[:, None]).astype(jnp.bfloat16).reshape(rows, heads, width)


def body(
    x_moe,
    routes,
    router_logits,
    w_gate,
    w_up,
    w_down,
    q_latent,
    q_rope,
    kv_latent,
    key_rope,
    prompt_lengths,
):
    n_ep = lax.axis_size("ep")
    local = w_gate.shape[0]
    experts = local * n_ep
    rows, top_k = routes.shape
    part_width = x_moe.shape[1]
    flat = routes.reshape(-1)
    onehot = (flat[:, None] == jnp.arange(experts, dtype=jnp.int32)[None, :]).astype(jnp.int32)
    rank = jnp.sum((jnp.cumsum(onehot, axis=0) - onehot) * onehot, axis=1)
    dest = flat * CAP + rank
    placing = (jnp.arange(experts * CAP, dtype=jnp.int32)[:, None] == dest[None, :]).astype(
        jnp.bfloat16
    )
    placing = jnp.sum(placing.reshape(experts * CAP, rows, top_k), axis=2)
    slots = n_ep * CAP
    full_rows = lax.all_gather(x_moe, "tp", axis=1, tiled=True)
    width = full_rows.shape[1]
    buffer = jnp.dot(placing, full_rows, preferred_element_type=jnp.float32).astype(jnp.bfloat16)
    arrived = lax.all_to_all(
        buffer.reshape(n_ep, local * CAP, width), "ep", split_axis=0, concat_axis=0, tiled=True
    )
    arranged = arrived.reshape(n_ep, local, CAP, width)
    slot_rows = jnp.transpose(arranged, (1, 0, 2, 3)).reshape(local, slots, width)
    gate_act = jnp.einsum("esd,edf->esf", slot_rows, w_gate, preferred_element_type=jnp.float32)
    up_act = jnp.einsum("esd,edf->esf", slot_rows, w_up, preferred_element_type=jnp.float32)
    hidden = (jax.nn.silu(gate_act) * up_act).astype(jnp.bfloat16)
    partial_value = jnp.einsum("esf,efd->esd", hidden, w_down, preferred_element_type=jnp.float32)
    summed = lax.psum_scatter(
        partial_value.astype(jnp.bfloat16), "tp", scatter_dimension=2, tiled=True
    )
    returning = jnp.transpose(summed.reshape(local, n_ep, CAP, part_width), (1, 0, 2, 3))
    returned = lax.all_to_all(
        returning.reshape(n_ep, local * CAP, part_width),
        "ep",
        split_axis=0,
        concat_axis=0,
        tiled=True,
    )
    picked = (
        returned.reshape(experts * CAP, part_width)[dest]
        .astype(jnp.float32)
        .reshape(rows, top_k, part_width)
    )
    probs = jax.nn.sigmoid(router_logits)
    gates = route_scale * probs / jnp.sum(probs, axis=1, keepdims=True)
    moe_out = jnp.sum(gates[:, :, None] * picked, axis=1).astype(jnp.bfloat16)
    context = attend(q_latent, q_rope, kv_latent, key_rope, prompt_lengths)
    return (moe_out, context)


def solution(mesh):
    in_specs = (
        P(("groups", "ep"), "tp"),
        P(("groups", "ep"), None),
        P(("groups", "ep"), None),
        P("ep", None, "tp"),
        P("ep", None, "tp"),
        P("ep", "tp", None),
        P(("groups", "ep"), "tp", None),
        P(("groups", "ep"), "tp"),
        P(("groups", "ep"), None),
        P(("groups", "ep"), None),
        P("groups"),
    )
    out_specs = (P(("groups", "ep"), "tp"), P(("groups", "ep"), "tp", None))
    return jax.shard_map(body, mesh=mesh, in_specs=in_specs, out_specs=out_specs, check_vma=False)
```

profile of v0, /device:TPU:0, one launch (start us, length us, event | category | flops | bytes accessed | tf_op | source)
XLA Modules:
  0.0 159.4 jit_solution(11691830931009895452)
XLA Ops:
  7.2 0.8 copy.20
  8.1 0.1 eq.45
  8.2 0.1 fusion.33
  8.3 0.2 reduce_window_sum.19
  8.5 0.2 select_reduce_fusion
  8.7 0.1 reduce_sum.72
  8.9 0.1 fusion.32
  9.0 23.1 %all_gather.9 = bf16[64,7168]{1,0:T(8,128)(2,1)S(1)} all-gather(bf16[64,1792]{1,0:T(8,128)(2,1)} %param.11), channel_id=1, replica_groups=mesh['groups'=2,'ep'=4,'tp'=4] {'tp'}, dimensions={1}, use_global_device_ids=true | all-gather | bytes 1146880 | tf_op jit(solution)/shard_map/all_gather | solution.py:73
  32.1 0.9 convolution_convert_fusion.1
  33.0 35.3 %all_to_all.10 = bf16[4,48,7168]{2,1,0:T(8,128)(2,1)S(1)} all-to-all(bf16[4,48,7168]{2,1,0:T(8,128)(2,1)S(1)} %bitcast.44), channel_id=1, replica_groups=mesh['groups'=2,'ep'=4,'tp'=4] {'ep'}, dimensions={0} | all-to-all | bytes 5505024 | tf_op jit(solution)/shard_map/all_to_all | solution.py:76
  68.3 1.6 copy-done.1
  69.8 1.6 fusion.4
  71.5 10.7 %fusion = bf16[1,192,7168]{2,1,0:T(8,128)(2,1)} fusion(bf16[1,512,7168]{2,1,0:T(8,128)(2,1)} %param.16, bf16[192,7168]{1,0:T(8,128)(2,1)} %bitcast.43, bf16[1,7168,512]{2,1,0:T(8,128)(2,1)} %param.15, f32[192,512]{1,0:T(8,128)S(1)} %fusion.4), kind=kOutput, calls=%fused_computation.3 | convolution fusion | flops 2820538368 | bytes 20578304 | tf_op jit(solution)/shard_map/esf,efd->esd/dot_general | solution.py:84
  82.3 0.1 mul.63
  82.4 0.2 reshape.144
  82.8 0.2 reduce-window.8
  82.9 0.1 convert_reduce_fusion.1
  83.1 0.1 eq.51
  83.2 5.2 %all_gather.11 = bf16[256,64]{1,0:T(8,128)(2,1)S(1)} all-gather(bf16[64,64]{1,0:T(8,128)(2,1)S(1)} %copy-done.4), channel_id=1, replica_groups=mesh['groups'=2,'ep'=4,'tp'=4] {'ep'}, dimensions={0}, use_global_device_ids=true | all-gather | bytes 40960 | tf_op jit(solution)/shard_map/all_gather | solution.py:29
  88.4 5.8 %all_gather.10 = bf16[256,512]{1,0:T(8,128)(2,1)S(1)} all-gather(bf16[64,512]{1,0:T(8,128)(2,1)S(1)} %copy-done.3), channel_id=1, replica_groups=mesh['groups'=2,'ep'=4,'tp'=4] {'ep'}, dimensions={0}, use_global_device_ids=true | all-gather | bytes 327680 | tf_op jit(solution)/shard_map/all_gather | solution.py:28
  94.3 0.1 convert_reduce_fusion
  94.4 0.5 fusion.40
  94.9 0.5 fusion.39
  95.4 39.8 %reduce-scatter.2.cloned.1.call-done = bf16[1,192,1792]{2,1,0:T(8,128)(2,1)} async-done(((bf16[1,192,7168]{2,1,0:T(8,128)(2,1)}), bf16[1,192,1792]{2,1,0:T(8,128)(2,1)}) %reduce-scatter.2.cloned.1.call-update) | async-done | bytes 688144 | tf_op jit(solution)/shard_map/reduce_scatter | solution.py:85
  135.2 3.5 %all-to-all-start.1 = ((bf16[4,48,1792]{2,1,0:T(8,128)(2,1)}), bf16[4,48,1792]{2,1,0:T(8,128)(2,1)S(1)}, u32[]{:S(2)}, u32[]{:S(2)}) async-start(bf16[4,48,1792]{2,1,0:T(8,128)(2,1)} %bitcast.45), calls=%async_computation.2 | async-start | bytes 1376256 | tf_op jit(solution)/shard_map/all_to_all | solution.py:89
  138.7 0.3 fusion.15
  139.0 0.1 copy.19
  139.1 1.6 %divide_convert_fusion = bf16[1024,512]{1,0:T(8,128)(2,1)} fusion(bf16[256,512]{1,0:T(8,128)(2,1)S(1)} %all_gather.10, f32[1024]{0:T(1024)S(1)} %fusion.15, f32[1024,256]{0,1:T(8,128)S(1)} %get-tuple-element.7, f32[1024]{0:T(1024)S(1)} %broadcast_maximum_fusion, s32[1024]{0:T(1024)S(1)} %le.16, s32[1024]{0:T(1024)S(1)} %eq.51, s32[256]{0:T(256)S(1)} %convert_reduce_fusion), kind=kOutput, calls=%fused_computation.9 | convolution fusion | flops 271056896 | bytes 2376704 | tf_op jit(solution)/shard_map/dot_general | solution.py:41
  140.7 8.5 %all-to-all-done.1 = bf16[4,48,1792]{2,1,0:T(8,128)(2,1)S(1)} async-done(((bf16[4,48,1792]{2,1,0:T(8,128)(2,1)}), bf16[4,48,1792]{2,1,0:T(8,128)(2,1)S(1)}, u32[]{:S(2)}, u32[]{:S(2)}) %all-to-all-start.1) | async-done | bytes 688160 | tf_op jit(solution)/shard_map/all_to_all | solution.py:89
  149.2 0.9 gather_fusion
  150.2 0.4 reshape.146
  150.6 2.0 %multiply_reduce_fusion = bf16[64,1792]{1,0:T(8,128)(2,1)} fusion(f32[64,2,1792]{2,1,0:T(2,128)S(1)} %reshape.146, f32[64,2]{1,0:T(8,128)S(1)} %copy.19), kind=kLoop, calls=%fused_computation.18 | loop fusion | flops 344064 | bytes 1147392 | tf_op jit(solution)/shard_map/reduce_sum | solution.py:103
  (28 shorter events, 0.5 us)
Async XLA Ops:
  7.2 87.2 %copy-start = (bf16[64,16,512]{2,1,0:T(8,128)(2,1)S(1)}, bf16[64,16,512]{2,1,0:T(8,128)(2,1)}, u32[]{:S(2)}) copy-start(bf16[64,16,512]{2,1,0:T(8,128)(2,1)} %param.17) | copy-start | bytes 3145732
  7.2 128.0 %reduce-scatter.2.cloned.1.call-start = ((), (), s32[]{:S(2)}) async-start(), calls=%async_computation.3 | async-start | bytes 3440640 | tf_op jit(solution)/shard_map/reduce_scatter | solution.py:85
  8.9 61.0 %copy-start.6 = (bf16[1,7168,512]{2,1,0:T(8,128)(2,1)S(1)}, bf16[1,7168,512]{2,1,0:T(8,128)(2,1)}, u32[]{:S(2)}) copy-start(bf16[1,7168,512]{2,1,0:T(8,128)(2,1)} %param.14) | copy-start | bytes 22020100
  68.3 1.6 copy-start.1
  71.4 11.0 %copy-start.2 = (bf16[64,1024]{1,0:T(8,128)(2,1)S(1)}, bf16[64,1024]{1,0:T(8,128)(2,1)}, u32[]{:S(2)}) copy-start(bf16[64,1024]{1,0:T(8,128)(2,1)} %param.18) | copy-start | bytes 393220
  71.4 11.3 %copy-start.7 = (s32[8]{0:T(128)S(1)}, s32[8]{0:T(128)}, u32[]{:S(2)}) copy-start(s32[8]{0:T(128)} %param.21) | copy-start | bytes 100
  71.5 11.7 %copy-start.4 = (bf16[64,64]{1,0:T(8,128)(2,1)S(1)}, bf16[64,64]{1,0:T(8,128)(2,1)}, u32[]{:S(2)}) copy-start(bf16[64,64]{1,0:T(8,128)(2,1)} %param.20) | copy-start | bytes 24580
  71.5 17.0 %copy-start.3 = (bf16[64,512]{1,0:T(8,128)(2,1)S(1)}, bf16[64,512]{1,0:T(8,128)(2,1)}, u32[]{:S(2)}) copy-start(bf16[64,512]{1,0:T(8,128)(2,1)} %param.19) | copy-start | bytes 196612
  71.5 22.9 %copy-start.5 = (f32[64,2]{0,1:T(2,128)S(1)}, f32[64,2]{0,1:T(2,128)}, u32[]{:S(2)}) copy-start(f32[64,2]{0,1:T(2,128)} %param.13) | copy-start | bytes 1540
  135.2 14.1 %all-to-all-start.1 = ((bf16[4,48,1792]{2,1,0:T(8,128)(2,1)}), bf16[4,48,1792]{2,1,0:T(8,128)(2,1)S(1)}, u32[]{:S(2)}, u32[]{:S(2)}) async-start(bf16[4,48,1792]{2,1,0:T(8,128)(2,1)} %bitcast.45), calls=%async_computation.2 | async-start | bytes 1376256 | tf_op jit(solution)/shard_map/all_to_all | solution.py:89
Sparse Core Ops, SparseCore 0:
  82.4 52.7 reduce-scatter.1
where the time goes:
time: 160 us; the launch traced here: 159 us
  blocking collectives  69.5 us (43%)
  waiting for transfers between devices  48.4 us (30%)
  matrix products  15.7 us (10%)
  between operations  14.2 us (9%)
  local copies, waits for them, and re-layouts  4.9 us (3%)
  starting transfers between devices  3.52 us (2%)
  other arithmetic  3.22 us (2%)
    reduce_scatter x1, waiting for transfers between devices, body(): lax.psum_scatter(partial_value.astype(jnp.bfloat16), 'tp', scatter_dimens...  39.8 us
    all_to_all x1, blocking collectives, body(): lax.all_to_all(buffer.reshape(n_ep, local * CAP, width), 'ep', split_axis...  35.3 us
    all_gather x1, blocking collectives, body(): full_rows = lax.all_gather(x_moe, 'tp', axis=1, tiled=True)  23.1 us
    dot_general x1, matrix products, body(): jnp.einsum('esf,efd->esd', hidden, w_down, preferred_element_type=jnp.flo...  10.7 us
    all_to_all x1, waiting for transfers between devices, body(): lax.all_to_all(returning.reshape(n_ep, local * CAP, part_width), 'ep', sp...  8.53 us
    all_gather x1, blocking collectives, attend(): keys = lax.all_gather(kv_latent, 'ep', axis=0, tiled=True)  5.84 us
    all_gather x1, blocking collectives, attend(): rot_keys = lax.all_gather(key_rope, 'ep', axis=0, tiled=True)  5.24 us
    all_to_all x1, starting transfers between devices, body(): lax.all_to_all(returning.reshape(n_ep, local * CAP, part_width), 'ep', sp...  3.48 us
  transfers between devices with their start and end apart: 2, of which 2 were waited for; matrix products, arithmetic and copies ran while one was open for 2% of the time, Pallas kernels for 0%

commit v1 on v0

v1 whole, which is shorter than its diff:
```python
import functools

import jax
import jax.numpy as jnp
from jax import lax
from jax.experimental import pallas as pl
from jax.experimental.pallas import tpu as pltpu
from jax.sharding import PartitionSpec as P

MESH = pl.DeviceIdType.MESH
score_scale = 192.0 ** (-0.5)
route_scale = 2.5
CORES = 2


def prompt_of(lengths, positions):
    ends = jnp.cumsum(lengths)
    return jnp.sum((positions[:, None] >= ends[None, :]).astype(jnp.int32), axis=1)


def kernel(
    n_ep,
    n_tp,
    x_ref,
    gt_ref,
    ql_ref,
    qr_ref,
    kv_ref,
    kr_ref,
    bias_ref,
    wg_ref,
    wu_ref,
    wd_ref,
    moe_ref,
    ctx_ref,
    xall,
    gall,
    keys,
    rots,
    wg,
    wu,
    wd,
    acc_g,
    acc_u,
    hid,
    gcol,
    part,
    from_core,
    from_x,
    from_z,
    zsend,
    w_sem,
    small_send,
    small_recv,
    zg_send,
    zg_recv,
    xg_send,
    xg_recv,
    cg_send,
    cg_recv,
    cr_send,
    cr_recv,
    xr_send,
    xr_recv,
    zr_send,
    zr_recv,
):
    n_x = n_ep // CORES
    me = lax.axis_index("ep")
    z = lax.axis_index("tp")
    core = me % CORES
    xx = me // CORES
    other = me + 1 - 2 * core
    rows, width = x_ref.shape
    hidden_units = wg.shape[1]
    tokens = n_ep * rows

    def remote(src, dst, send, recv, ep=None, tp=None):
        where = {}
        if ep is not None:
            where["ep"] = ep
        if tp is not None:
            where["tp"] = tp
        return pltpu.make_async_remote_copy(
            src_ref=src, dst_ref=dst, send_sem=send, recv_sem=recv, device_id=where, device_id_type=MESH
        )

    def ep_peer(step):
        return lax.rem(me + step, n_ep)

    def x_of(step):
        return lax.rem(xx + step, n_x)

    def w_copies(b):
        span = pl.ds(pl.multiple_of(b * width, width), width)
        return (
            pltpu.make_async_copy(wg_ref.at[0, span, :], wg.at[span, :], w_sem.at[0, b]),
            pltpu.make_async_copy(wu_ref.at[0, span, :], wu.at[span, :], w_sem.at[1, b]),
            pltpu.make_async_copy(
                wd_ref.at[0, :, pl.ds(pl.multiple_of(b * width, 128), width)], wd.at[b], w_sem.at[2, b]
            ),
        )

    def sides(d):
        if d == 0:
            return [(None, z)]
        return [(z >= d, z - d), (z + d < n_tp, z + d)]

    def on(cond, fn):
        if cond is None:
            fn()
        else:
            pl.when(cond)(fn)

    def start_w(d, which):
        for cond, b in sides(d):

            def go(b=b):
                for i in which:
                    w_copies(b)[i].start()

            on(cond, go)

    barrier = pltpu.get_barrier_semaphore()
    for s in range(1, n_ep):
        pl.semaphore_signal(barrier, inc=1, device_id={"ep": ep_peer(s)}, device_id_type=MESH)

    @pl.when(z > 0)
    def _():
        pl.semaphore_signal(barrier, inc=1, device_id={"tp": z - 1}, device_id_type=MESH)

    @pl.when(z < n_tp - 1)
    def _():
        pl.semaphore_signal(barrier, inc=1, device_id={"tp": z + 1}, device_id_type=MESH)

    for d in range(n_tp):
        start_w(d, (0, 1))
    for d in range(n_tp - 1, -1, -1):
        start_w(d, (2,))

    edge = (z == 0) | (z == n_tp - 1)

    @pl.when(edge)
    def _():
        pl.semaphore_wait(barrier, n_ep)

    @pl.when(jnp.logical_not(edge))
    def _():
        pl.semaphore_wait(barrier, n_ep + 1)

    def gate_copy(s):
        return remote(gt_ref, gall.at[me], small_send.at[0, s], small_recv.at[0, s], ep=ep_peer(s))

    def gate_arrival(s):
        src = lax.rem(me + n_ep - s, n_ep)
        return remote(gt_ref, gall.at[src], small_send.at[0, s], small_recv.at[0, s], ep=ep_peer(s))

    def key_x(s):
        dst = x_of(s) * CORES + core
        return (
            remote(kv_ref, keys.at[me], small_send.at[1, s], small_recv.at[1, s], ep=dst),
            remote(kr_ref, rots.at[me], small_send.at[2, s], small_recv.at[2, s], ep=dst),
        )

    def key_core(s, owner, own):
        src_kv = kv_ref if own else keys.at[owner]
        src_kr = kr_ref if own else rots.at[owner]
        return (
            remote(src_kv, keys.at[owner], small_send.at[3, s], small_recv.at[3, s], ep=other),
            remote(src_kr, rots.at[owner], small_send.at[4, s], small_recv.at[4, s], ep=other),
        )

    for s in range(1, n_x):
        for c in key_x(s):
            c.start()
    for c in key_core(0, me, True):
        c.start()
    for s in range(1, n_ep):
        gate_copy(s).start()

    def zg(direction, b, own):
        to = z + 1 if direction == 0 else z - 1
        return remote(
            x_ref if own else xall.at[b, me],
            xall.at[b, me],
            zg_send.at[direction, b],
            zg_recv.at[direction, b],
            tp=to,
        )

    def xg(s, b, own):
        return remote(
            x_ref if own else xall.at[b, me],
            xall.at[b, me],
            xg_send.at[s, b],
            xg_recv.at[s, b],
            ep=x_of(s) * CORES + core,
        )

    def xg_in(s, b):
        src = lax.rem(xx + n_x - s, n_x) * CORES + core
        return remote(xall.at[b, src], xall.at[b, src], xg_send.at[s, b], xg_recv.at[s, b], ep=src), src

    def cg(s, b, owner, own):
        return remote(
            x_ref if own else xall.at[b, owner],
            xall.at[b, owner],
            cg_send.at[s, b],
            cg_recv.at[s, b],
            ep=other,
        )

    def cg_in(s, b):
        src = lax.rem(xx + n_x - s, n_x) * CORES + 1 - core
        return remote(xall.at[b, src], xall.at[b, src], cg_send.at[s, b], cg_recv.at[s, b], ep=other)

    def spread(b, own):
        for s in range(1, n_x):
            xg(s, b, own).start()
        cg(0, b, me, own).start()

    @pl.when(z < n_tp - 1)
    def _():
        zg(0, z, True).start()

    @pl.when(z > 0)
    def _():
        zg(1, z, True).start()

    spread(z, True)
    xall[z, me] = x_ref[...]
    keys[me] = kv_ref[...]
    rots[me] = kr_ref[...]
    gall[me] = gt_ref[...]
    acc_g[...] = jnp.zeros_like(acc_g)
    acc_u[...] = jnp.zeros_like(acc_u)

    for s in range(1, n_x):
        src = lax.rem(xx + n_x - s, n_x) * CORES + core
        for c in key_x(s):
            c.wait_recv()
        for c in key_core(s, src, False):
            c.start()
    for s in range(n_x):
        src = lax.rem(xx + n_x - s, n_x) * CORES + 1 - core
        for c in key_core(s, src, False):
            c.wait_recv()

    heads = ql_ref.shape[0] // rows
    block_tokens = 16
    block = block_tokens * heads

    def attend(i, carry):
        at = pl.multiple_of(i * block, block)
        all_keys = keys[...].reshape(tokens, keys.shape[2])
        all_rots = rots[...].reshape(tokens, rots.shape[2])
        dims = (((1,), (1,)), ((), ()))
        scores = lax.dot_general(
            ql_ref[pl.ds(at, block), :], all_keys, dims, preferred_element_type=jnp.float32
        )
        scores += lax.dot_general(
            qr_ref[pl.ds(at, block), :], all_rots, dims, preferred_element_type=jnp.float32
        )
        bias = bias_ref[pl.ds(pl.multiple_of(i * block_tokens, block_tokens), block_tokens), :]
        bias = jnp.broadcast_to(bias[:, None, :], (block_tokens, heads, tokens)).reshape(block, tokens)
        masked = jnp.where(bias < 0.0, -1e30, scores * score_scale)
        top = jnp.max(masked, axis=1, keepdims=True)
        weights = jnp.where(bias < 0.0, 0.0, jnp.exp(masked - top))
        total = jnp.sum(weights, axis=1, keepdims=True)
        out = jnp.dot(weights.astype(jnp.bfloat16), all_keys, preferred_element_type=jnp.float32)
        ctx_ref[pl.ds(at, block), :] = (out / total).astype(jnp.bfloat16)
        return carry

    lax.fori_loop(0, rows // block_tokens, attend, 0)

    tile = 256

    def multiply(b):
        for i in (0, 1):
            w_copies(b)[i].wait()
        span = pl.ds(pl.multiple_of(b * width, width), width)

        def column(j, carry):
            cols = pl.ds(pl.multiple_of(j * tile, tile), tile)
            x = xall[b].reshape(tokens, width)
            acc_g[:, cols] += jnp.dot(x, wg[span, cols], preferred_element_type=jnp.float32)
            acc_u[:, cols] += jnp.dot(x, wu[span, cols], preferred_element_type=jnp.float32)
            return carry

        lax.fori_loop(0, hidden_units // tile, column, 0)

    def process(b):
        for s in range(1, n_x):
            arrival, src = xg_in(s, b)
            arrival.wait_recv()
            cg(s, b, src, False).start()
        for s in range(n_x):
            cg_in(s, b).wait_recv()
        multiply(b)

    for d in range(1, n_tp + 1):
        if d < n_tp:

            @pl.when(z >= d)
            def _():
                b = z - d
                zg(0, b, False).wait_recv()

                @pl.when(z < n_tp - 1)
                def _():
                    zg(0, b, False).start()

                spread(b, False)

            @pl.when(z + d < n_tp)
            def _():
                b = z + d
                zg(1, b, False).wait_recv()

                @pl.when(z > 0)
                def _():
                    zg(1, b, False).start()

                spread(b, False)

        for cond, b in sides(d - 1):
            on(cond, functools.partial(process, b))

    gate_act = acc_g[...]
    hid[...] = (gate_act / (1.0 + jnp.exp(-gate_act)) * acc_u[...]).astype(jnp.bfloat16)
    for s in range(1, n_ep):
        gate_arrival(s).wait_recv()
    experts = gall.shape[1]
    mine = lax.broadcasted_iota(jnp.int32, (experts, 128), 0) == me

    for e in range(n_ep):
        row = jnp.sum(jnp.where(mine, gall[e], 0.0), axis=0, keepdims=True)
        square = jnp.broadcast_to(row, (128, 128)).T
        gcol[e * rows : (e + 1) * rows, :] = square[:rows, :]

    def cr(s, b):
        owner = x_of(s) * CORES + 1 - core
        return remote(part.at[b, owner], from_core.at[s, b], cr_send.at[s, b], cr_recv.at[s, b], ep=other)

    def xr(s, b):
        dst = x_of(s) * CORES + core
        return remote(part.at[b, dst], from_x.at[s - 1, b], xr_send.at[s, b], xr_recv.at[s, b], ep=dst)

    down_tile = 256 if width % 256 == 0 else 128

    def down(b):
        w_copies(b)[2].wait()

        def column(j, carry):
            cols = pl.ds(pl.multiple_of(j * down_tile, down_tile), down_tile)
            out = jnp.dot(hid[...], wd[b, :, cols], preferred_element_type=jnp.float32)
            out = (out * gcol[:, :1]).astype(jnp.bfloat16)
            part[b, :, :, cols] = out.reshape(n_ep, rows, down_tile)
            return carry

        lax.fori_loop(0, width // down_tile, column, 0)
        for s in range(1, n_x):
            cr(s, b).start()
        cr(0, b).start()

    def over_x(b):
        for s in range(1, n_x):
            dst = x_of(s) * CORES + core
            cr(s, b).wait_recv()
            part[b, dst] = (
                part[b, dst].astype(jnp.float32) + from_core[s, b].astype(jnp.float32)
            ).astype(jnp.bfloat16)
            xr(s, b).start()

    for d in range(n_tp - 1, -2, -1):
        if d >= 0:
            for cond, b in sides(d):
                on(cond, functools.partial(down, b))
        if d + 1 < n_tp:
            for cond, b in sides(d + 1):
                on(cond, functools.partial(over_x, b))

    def zr(direction, b):
        to = z + 1 if direction == 0 else z - 1
        return remote(
            zsend.at[b], from_z.at[direction, b], zr_send.at[b], zr_recv.at[direction, b], tp=to
        )

    def chip_sum(b):
        cr(0, b).wait_recv()
        total = part[b, me].astype(jnp.float32) + from_core[0, b].astype(jnp.float32)
        for s in range(1, n_x):
            xr(s, b).wait_recv()
            total += from_x[s - 1, b].astype(jnp.float32)
        return total

    def along(direction, b, first):
        @pl.when(first)
        def _():
            zsend[b] = chip_sum(b).astype(jnp.bfloat16)

        @pl.when(jnp.logical_not(first))
        def _():
            zr(direction, b).wait_recv()
            zsend[b] = (chip_sum(b) + from_z[direction, b].astype(jnp.float32)).astype(jnp.bfloat16)

        zr(direction, b).start()

    for d in range(n_tp - 1, 0, -1):
        pl.when(z >= d)(functools.partial(along, 1, z - d, z == n_tp - 1))
        pl.when(z + d < n_tp)(functools.partial(along, 0, z + d, z == 0))

    zsum = acc_final = chip_sum(z)

    @pl.when(z == 0)
    def _():
        zr(1, z).wait_recv()
        moe_ref[...] = (acc_final + from_z[1, z].astype(jnp.float32)).astype(jnp.bfloat16)

    @pl.when(z == n_tp - 1)
    def _():
        zr(0, z).wait_recv()
        moe_ref[...] = (acc_final + from_z[0, z].astype(jnp.float32)).astype(jnp.bfloat16)

    @pl.when((z > 0) & (z < n_tp - 1))
    def _():
        zr(0, z).wait_recv()
        zr(1, z).wait_recv()
        moe_ref[...] = (
            zsum + from_z[0, z].astype(jnp.float32) + from_z[1, z].astype(jnp.float32)
        ).astype(jnp.bfloat16)

    for s in range(1, n_ep):
        gate_copy(s).wait_send()
    for s in range(1, n_x):
        for c in key_x(s):
            c.wait_send()
    for s in range(n_x):
        for c in key_core(s, me, True):
            c.wait_send()

    def drain(b, own):
        for s in range(1, n_x):
            xg(s, b, own).wait_send()
            xr(s, b).wait_send()
        for s in range(n_x):
            cg(s, b, me, False).wait_send()
            cr(s, b).wait_send()

    for d in range(n_tp):
        for cond, b in sides(d):
            on(cond, functools.partial(drain, b, d == 0))

    @pl.when(z < n_tp - 1)
    def _():
        zg(0, z, True).wait_send()

    @pl.when(z > 0)
    def _():
        zg(1, z, True).wait_send()

    for d in range(1, n_tp):

        @pl.when((z >= d) & (z < n_tp - 1))
        def _():
            zg(0, z - d, False).wait_send()

        @pl.when((z + d < n_tp) & (z > 0))
        def _():
            zg(1, z + d, False).wait_send()

        @pl.when(z >= d)
        def _():
            zr(1, z - d).wait_send()

        @pl.when(z + d < n_tp)
        def _():
            zr(0, z + d).wait_send()


def body(
    x_moe,
    routes,
    router_logits,
    w_gate,
    w_up,
    w_down,
    q_latent,
    q_rope,
    kv_latent,
    key_rope,
    prompt_lengths,
):
    n_ep = lax.axis_size("ep")
    n_tp = lax.axis_size("tp")
    n_x = n_ep // CORES
    rows, width = x_moe.shape
    _, heads, latent = q_latent.shape
    rope = key_rope.shape[1]
    units = w_gate.shape[2]
    tokens = n_ep * rows
    experts = max(8, n_ep)

    probs = jax.nn.sigmoid(router_logits)
    gates = route_scale * probs / jnp.sum(probs, axis=1, keepdims=True)
    names = jnp.arange(experts, dtype=jnp.int32)[:, None, None]
    table = jnp.sum(jnp.where(routes[None] == names, gates[None], 0.0), axis=2)
    table = jnp.pad(table, ((0, 0), (0, 128 - rows)))

    q_pos = lax.axis_index("ep") * rows + jnp.arange(rows, dtype=jnp.int32)
    k_pos = jnp.arange(tokens, dtype=jnp.int32)
    q_prompt = prompt_of(prompt_lengths, q_pos)
    k_prompt = prompt_of(prompt_lengths, k_pos)
    visible = (q_prompt[:, None] == k_prompt[None, :]) & (k_pos[None, :] <= q_pos[:, None])
    bias = jnp.where(visible, 0.0, -1.0).astype(jnp.float32)

    vmem = pl.BlockSpec(memory_space=pltpu.VMEM)
    hbm = pl.BlockSpec(memory_space=pl.ANY)
    bf16, f32 = jnp.bfloat16, jnp.float32
    dma = pltpu.SemaphoreType.DMA
    moe, ctx = pl.pallas_call(
        functools.partial(kernel, n_ep, n_tp),
        out_shape=(
            jax.ShapeDtypeStruct((rows, width), bf16),
            jax.ShapeDtypeStruct((rows * heads, latent), bf16),
        ),
        in_specs=[vmem] * 7 + [hbm] * 3,
        out_specs=(vmem, vmem),
        scratch_shapes=[
            pltpu.VMEM((n_tp, n_ep, rows, width), bf16),
            pltpu.VMEM((n_ep, experts, 128), f32),
            pltpu.VMEM((n_ep, rows, latent), bf16),
            pltpu.VMEM((n_ep, rows, rope), bf16),
            pltpu.VMEM((n_tp * width, units), bf16),
            pltpu.VMEM((n_tp * width, units), bf16),
            pltpu.VMEM((n_tp, units, width), bf16),
            pltpu.VMEM((tokens, units), f32),
            pltpu.VMEM((tokens, units), f32),
            pltpu.VMEM((tokens, units), bf16),
            pltpu.VMEM((tokens, 128), f32),
            pltpu.VMEM((n_tp, n_ep, rows, width), bf16),
            pltpu.VMEM((n_x, n_tp, rows, width), bf16),
            pltpu.VMEM((n_x - 1, n_tp, rows, width), bf16),
            pltpu.VMEM((2, n_tp, rows, width), bf16),
            pltpu.VMEM((n_tp, rows, width), bf16),
            dma((3, n_tp)),
            dma((5, n_ep)),
            dma((5, n_ep)),
            dma((2, n_tp)),
            dma((2, n_tp)),
            dma((n_x, n_tp)),
            dma((n_x, n_tp)),
            dma((n_x, n_tp)),
            dma((n_x, n_tp)),
            dma((n_x, n_tp)),
            dma((n_x, n_tp)),
            dma((n_x, n_tp)),
            dma((n_x, n_tp)),
            dma((n_tp,)),
            dma((2, n_tp)),
        ],
        compiler_params=pltpu.CompilerParams(
            collective_id=0, has_side_effects=True, vmem_limit_bytes=62 * 1024 * 1024
        ),
        name="layer",
    )(
        x_moe,
        table,
        q_latent.reshape(rows * heads, latent),
        q_rope.reshape(rows * heads, rope),
        kv_latent,
        key_rope,
        bias,
        w_gate,
        w_up,
        w_down,
    )
    return moe, ctx.reshape(rows, heads, latent)


def solution(mesh):
    in_specs = (
        P(("groups", "ep"), "tp"),
        P(("groups", "ep"), None),
        P(("groups", "ep"), None),
        P("ep", None, "tp"),
        P("ep", None, "tp"),
        P("ep", "tp", None),
        P(("groups", "ep"), "tp", None),
        P(("groups", "ep"), "tp"),
        P(("groups", "ep"), None),
        P(("groups", "ep"), None),
        P("groups"),
    )
    out_specs = (P(("groups", "ep"), "tp"), P(("groups", "ep"), "tp", None))
    return jax.shard_map(body, mesh=mesh, in_specs=in_specs, out_specs=out_specs, check_vma=False)
```

time: 160 us -> 79 us (0.49)
  blocking collectives: 69.5 us -> 0 us
  Pallas kernels: 0 us -> 68.7 us
  waiting for transfers between devices: 48.4 us -> 0 us
  matrix products: 15.7 us -> 0 us
  between operations: 14.2 us -> 0.65 us
  starting transfers between devices: 3.52 us -> 0 us
    pallas_call x0 -> x1, Pallas kernels: none -> 68.7 us  [body(): pl.pallas_call(functools.partial(kernel, n_ep, n_tp), out_shape=(jax.Shap...]
    reduce_scatter x1 -> x0, waiting for transfers between devices: 39.8 us -> none  [body(): lax.psum_scatter(partial_value.astype(jnp.bfloat16), 'tp', scatter_dimens...]
    all_to_all x1 -> x0, blocking collectives: 35.3 us -> none  [body(): lax.all_to_all(buffer.reshape(n_ep, local * CAP, width), 'ep', split_axis...]
    all_gather x3 -> x0, blocking collectives: 34.2 us -> none  [the longest x1 23.1 us: body(): full_rows = lax.all_gather(x_moe, 'tp', axis=1, tiled=True)]
    dot_general x6 -> x0, matrix products: 15.7 us -> none  [the longest x1 10.7 us: body(): jnp.einsum('esf,efd->esd', hidden, w_down, preferred_element_type=jnp.flo...]
    all_to_all x1 -> x0, waiting for transfers between devices: 8.53 us -> none  [body(): lax.all_to_all(returning.reshape(n_ep, local * CAP, part_width), 'ep', sp...]
    all_to_all x1 -> x0, starting transfers between devices: 3.48 us -> none  [body(): lax.all_to_all(returning.reshape(n_ep, local * CAP, part_width), 'ep', sp...]
    reduce_sum x4 -> x1, other arithmetic: 2.55 us -> 0.7 us  [body(): table = jnp.sum(jnp.where(routes[None] == names, gates[None], 0.0), axis=2)]
  transfers between devices with their start and end apart: 2 -> 0, of which waited for: 2 -> 0; matrix products, arithmetic and copies ran while one was open for 2% -> 0% of each run, Pallas kernels for 0% -> 0%
where the time goes in v1:
time: 79 us; the launch traced here: 78.8 us
  Pallas kernels  68.7 us (87%)
  local copies, waits for them, and re-layouts  6.32 us (8%)
  other arithmetic  3.13 us (4%)
    pallas_call x1, Pallas kernels, body(): pl.pallas_call(functools.partial(kernel, n_ep, n_tp), out_shape=(jax.Shap...  68.7 us
    unnamed x2, local copies, waits for them, and re-layouts  3.9 us
    reshape x1, local copies, waits for them, and re-layouts, body(): q_rope.reshape(rows * heads, rope)  1.82 us

profile of v1, /device:TPU:0, one launch (start us, length us, event | category | flops | bytes accessed | tf_op | source)
XLA Modules:
  0.0 78.8 jit_solution(14168395251782078325)
XLA Ops:
  0.6 0.8 %reduce-window.8 = s32[8,1]{0,1:T(1,128)S(1)} reduce-window(s32[8,1]{0,1:T(1,128)} %bitcast.6, s32[]{:T(128)} %constant.20.clone.1), window={size=8x1 pad=7_0x0_0}, to_apply=%region_2.3 | reduce-window | flops 56 | bytes 68 | tf_op jit(solution)/shard_map/reduce-window.3
  1.5 0.1 convert_reduce_fusion.1
  1.6 0.1 convert_reduce_fusion
  1.6 0.7 fusion.2
  2.4 0.7 select_reduce_fusion
  3.1 0.6 pad.4.gt_ref
  3.7 0.7 fusion.1.bias_ref
  4.4 1.8 %reshape.47.qr_ref = bf16[1024,64]{1,0:T(8,128)(2,1)} reshape(bf16[64,1024]{1,0:T(8,128)(2,1)} %param.18) | data formatting | bytes 262144 | tf_op jit(solution)/shard_map/reshape | solution.py:570
  6.2 68.7 %layer.1 = (bf16[64,1792]{1,0:T(8,128)(2,1)}, bf16[1024,512]{1,0:T(8,128)(2,1)}) custom-call(bf16[64,1792]{1,0:T(8,128)(2,1)} %x_ref.1, f32[8,128]{1,0:T(8,128)} %pad.4.gt_ref, bf16[1024,512]{1,0:T(8,128)(2,1)} %bitcast.4, bf16[1024,64]{1,0:T(8,128)(2,1)} %reshape.47.qr_ref, bf16[64,512]{1,0:T(8,128)(2,1)} %kv_ref.1, bf16[64,64]{1,0:T(8,128)(2,1)} %kr_ref.1, ...), custom_call_target="tpu_custom_call" | custom-call | tf_op jit(solution)/shard_map/layer/pallas_call | solution.py:521
  74.9 1.6 %copy.19 = bf16[64,1792]{1,0:T(8,128)(2,1)} copy(bf16[64,1792]{1,0:T(8,128)(2,1)} %get-tuple-element.10) | data formatting | bytes 458752
  76.5 2.3 %copy.20 = bf16[64,16,512]{2,1,0:T(8,128)(2,1)} copy(bf16[64,16,512]{2,1,0:T(8,128)(2,1)} %bitcast.5) | data formatting | bytes 2097152
  (2 shorter events, 0.0 us)

commit v2 on v1

--- a/solution.py
+++ b/solution.py
@@ -13,28 +13,27 @@
 CORES = 2
 
 
-def prompt_of(lengths, positions):
-    ends = jnp.cumsum(lengths)
-    return jnp.sum((positions[:, None] >= ends[None, :]).astype(jnp.int32), axis=1)
-
-
 def kernel(
     n_ep,
     n_tp,
     x_ref,
-    gt_ref,
+    routes_ref,
+    logits_ref,
     ql_ref,
     qr_ref,
     kv_ref,
     kr_ref,
-    bias_ref,
+    lengths_ref,
     wg_ref,
     wu_ref,
     wd_ref,
     moe_ref,
     ctx_ref,
     xall,
+    gt_ref,
     gall,
+    rope_keys,
+    hidden_from,
     keys,
     rots,
     wg,
@@ -48,7 +47,6 @@
     from_core,
     from_x,
     from_z,
-    zsend,
     w_sem,
     small_send,
     small_recv,
@@ -133,10 +131,14 @@
     def _():
         pl.semaphore_signal(barrier, inc=1, device_id={"tp": z + 1}, device_id_type=MESH)
 
-    for d in range(n_tp):
-        start_w(d, (0, 1))
-    for d in range(n_tp - 1, -1, -1):
-        start_w(d, (2,))
+    probs = 1.0 / (1.0 + jnp.exp(-logits_ref[...]))
+    gates = route_scale * probs / jnp.sum(probs, axis=1, keepdims=True)
+    lanes = lax.broadcasted_iota(jnp.int32, (rows, 128), 1)
+    table = jnp.zeros((rows, 128), jnp.float32)
+    for k in range(routes_ref.shape[1]):
+        table += jnp.where(routes_ref[:, k : k + 1] == lanes, gates[:, k : k + 1], 0.0)
+    square = jnp.concatenate([table, jnp.zeros((128 - rows, 128), jnp.float32)], axis=0)
+    gt_ref[...] = square.T[: gt_ref.shape[0], :]
 
     edge = (z == 0) | (z == n_tp - 1)
 
@@ -169,14 +171,6 @@
             remote(src_kv, keys.at[owner], small_send.at[3, s], small_recv.at[3, s], ep=other),
             remote(src_kr, rots.at[owner], small_send.at[4, s], small_recv.at[4, s], ep=other),
         )
-
-    for s in range(1, n_x):
-        for c in key_x(s):
-            c.start()
-    for c in key_core(0, me, True):
-        c.start()
-    for s in range(1, n_ep):
-        gate_copy(s).start()
 
     def zg(direction, b, own):
         to = z + 1 if direction == 0 else z - 1
@@ -228,6 +222,16 @@
         zg(1, z, True).start()
 
     spread(z, True)
+    for s in range(1, n_x):
+        for c in key_x(s):
+            c.start()
+    for c in key_core(0, me, True):
+        c.start()
+    for s in range(1, n_ep):
+        gate_copy(s).start()
+
+    for d in range(n_tp):
+        start_w(d, (0, 1))
     xall[z, me] = x_ref[...]
     keys[me] = kv_ref[...]
     rots[me] = kr_ref[...]
@@ -235,33 +239,165 @@
     acc_g[...] = jnp.zeros_like(acc_g)
     acc_u[...] = jnp.zeros_like(acc_u)
 
-    for s in range(1, n_x):
-        src = lax.rem(xx + n_x - s, n_x) * CORES + core
-        for c in key_x(s):
-            c.wait_recv()
-        for c in key_core(s, src, False):
-            c.start()
+
+    tile = 256
+
+    def multiply(b):
+        for i in (0, 1):
+            w_copies(b)[i].wait()
+        span = pl.ds(pl.multiple_of(b * width, width), width)
+
+        def column(j, carry):
+            cols = pl.ds(pl.multiple_of(j * tile, tile), tile)
+            x = xall[b].reshape(tokens, width)
+            acc_g[:, cols] += jnp.dot(x, wg[span, cols], preferred_element_type=jnp.float32)
+            acc_u[:, cols] += jnp.dot(x, wu[span, cols], preferred_element_type=jnp.float32)
+            return carry
+
+        lax.fori_loop(0, hidden_units // tile, column, 0)
+
+    def process(b):
+        for s in range(1, n_x):
+            arrival, src = xg_in(s, b)
+            arrival.wait_recv()
+            cg(s, b, src, False).start()
+        for s in range(n_x):
+            cg_in(s, b).wait_recv()
+        multiply(b)
+
+    for d in range(1, n_tp + 1):
+        if d < n_tp:
+
+            @pl.when(z >= d)
+            def _():
+                b = z - d
+                zg(0, b, False).wait_recv()
+
+                @pl.when(z < n_tp - 1)
+                def _():
+                    zg(0, b, False).start()
+
+                spread(b, False)
+
+            @pl.when(z + d < n_tp)
+            def _():
+                b = z + d
+                zg(1, b, False).wait_recv()
+
+                @pl.when(z > 0)
+                def _():
+                    zg(1, b, False).start()
+
+                spread(b, False)
+
+        if d == 2:
+            for far in range(n_tp - 1, -1, -1):
+                start_w(far, (2,))
+            for s in range(1, n_x):
+                src = lax.rem(xx + n_x - s, n_x) * CORES + core
+                for c in key_x(s):
+                    c.wait_recv()
+                for c in key_core(s, src, False):
+                    c.start()
+        for cond, b in sides(d - 1):
+            on(cond, functools.partial(process, b))
+
+    gate_act = acc_g[...]
+    hid[...] = (gate_act / (1.0 + jnp.exp(-gate_act)) * acc_u[...]).astype(jnp.bfloat16)
+    for s in range(1, n_ep):
+        gate_arrival(s).wait_recv()
+    experts = gall.shape[1]
+    mine = lax.broadcasted_iota(jnp.int32, (experts, 128), 0) == me
+
+    for e in range(n_ep):
+        row = jnp.sum(jnp.where(mine, gall[e], 0.0), axis=0, keepdims=True)
+        square = jnp.broadcast_to(row, (128, 128)).T
+        gcol[e * rows : (e + 1) * rows, :] = square[:rows, :]
+
+    def cr(s, b):
+        owner = x_of(s) * CORES + 1 - core
+        return remote(part.at[b, owner], from_core.at[s, b], cr_send.at[s, b], cr_recv.at[s, b], ep=other)
+
+    def xr(s, b):
+        dst = x_of(s) * CORES + core
+        return remote(part.at[b, dst], from_x.at[s - 1, b], xr_send.at[s, b], xr_recv.at[s, b], ep=dst)
+
+    down_tile = 256 if width % 256 == 0 else 128
+
+    def down(b):
+        w_copies(b)[2].wait()
+
+        def column(j, carry):
+            cols = pl.ds(pl.multiple_of(j * down_tile, down_tile), down_tile)
+            out = jnp.dot(hid[...], wd[b, :, cols], preferred_element_type=jnp.float32)
+            out = (out * gcol[:, :1]).astype(jnp.bfloat16)
+            part[b, :, :, cols] = out.reshape(n_ep, rows, down_tile)
+            return carry
+
+        lax.fori_loop(0, width // down_tile, column, 0)
+        for s in range(1, n_x):
+            cr(s, b).start()
+        cr(0, b).start()
+
+    def over_x(b):
+        for s in range(1, n_x):
+            dst = x_of(s) * CORES + core
+            cr(s, b).wait_recv()
+            part[b, dst] = (
+                part[b, dst].astype(jnp.float32) + from_core[s, b].astype(jnp.float32)
+            ).astype(jnp.bfloat16)
+            xr(s, b).start()
+
+    for d in range(n_tp - 1, -2, -1):
+        now = sides(d) if d >= 0 else []
+        before = sides(d + 1) if d + 1 < n_tp else []
+        for cond, b in now[:1]:
+            on(cond, functools.partial(down, b))
+        for cond, b in before:
+            on(cond, functools.partial(over_x, b))
+        for cond, b in now[1:]:
+            on(cond, functools.partial(down, b))
+
     for s in range(n_x):
         src = lax.rem(xx + n_x - s, n_x) * CORES + 1 - core
         for c in key_core(s, src, False):
             c.wait_recv()
 
     heads = ql_ref.shape[0] // rows
+    rope = rots.shape[2]
     block_tokens = 16
     block = block_tokens * heads
+    for e in range(n_ep):
+        rope_keys[e * rows : (e + 1) * rows, :] = jnp.concatenate([rots[e]] * heads, axis=1)
+
+    q_pos = me * rows + lax.broadcasted_iota(jnp.int32, (rows, tokens), 0)
+    k_pos = lax.broadcasted_iota(jnp.int32, (rows, tokens), 1)
+    q_prompt = jnp.zeros((rows, tokens), jnp.int32)
+    k_prompt = jnp.zeros((rows, tokens), jnp.int32)
+    end = jnp.int32(0)
+    for doc in range(lengths_ref.shape[0]):
+        end = end + lengths_ref[doc]
+        q_prompt += (q_pos >= end).astype(jnp.int32)
+        k_prompt += (k_pos >= end).astype(jnp.int32)
+    hidden_from[...] = jnp.where((q_prompt == k_prompt) & (k_pos <= q_pos), 0.0, -1.0)
+
+    spread_of = (block_tokens, heads, heads * rope)
+    own_lanes = (
+        lax.broadcasted_iota(jnp.int32, spread_of, 2) // rope == lax.broadcasted_iota(jnp.int32, spread_of, 1)
+    )
 
     def attend(i, carry):
         at = pl.multiple_of(i * block, block)
+        token_at = pl.ds(pl.multiple_of(i * block_tokens, block_tokens), block_tokens)
         all_keys = keys[...].reshape(tokens, keys.shape[2])
-        all_rots = rots[...].reshape(tokens, rots.shape[2])
         dims = (((1,), (1,)), ((), ()))
+        rotary = jnp.broadcast_to(qr_ref[token_at, :].astype(jnp.float32)[:, None, :], spread_of)
+        rotary = jnp.where(own_lanes, rotary, 0.0).reshape(block, heads * rope).astype(jnp.bfloat16)
         scores = lax.dot_general(
             ql_ref[pl.ds(at, block), :], all_keys, dims, preferred_element_type=jnp.float32
         )
-        scores += lax.dot_general(
-            qr_ref[pl.ds(at, block), :], all_rots, dims, preferred_element_type=jnp.float32
-        )
-        bias = bias_ref[pl.ds(pl.multiple_of(i * block_tokens, block_tokens), block_tokens), :]
+        scores += lax.dot_general(rotary, rope_keys[...], dims, preferred_element_type=jnp.float32)
+        bias = hidden_from[token_at, :]
         bias = jnp.broadcast_to(bias[:, None, :], (block_tokens, heads, tokens)).reshape(block, tokens)
         masked = jnp.where(bias < 0.0, -1e30, scores * score_scale)
         top = jnp.max(masked, axis=1, keepdims=True)
@@ -273,117 +409,10 @@
 
     lax.fori_loop(0, rows // block_tokens, attend, 0)
 
-    tile = 256
-
-    def multiply(b):
-        for i in (0, 1):
-            w_copies(b)[i].wait()
-        span = pl.ds(pl.multiple_of(b * width, width), width)
-
-        def column(j, carry):
-            cols = pl.ds(pl.multiple_of(j * tile, tile), tile)
-            x = xall[b].reshape(tokens, width)
-            acc_g[:, cols] += jnp.dot(x, wg[span, cols], preferred_element_type=jnp.float32)
-            acc_u[:, cols] += jnp.dot(x, wu[span, cols], preferred_element_type=jnp.float32)
-            return carry
-
-        lax.fori_loop(0, hidden_units // tile, column, 0)
-
-    def process(b):
-        for s in range(1, n_x):
-            arrival, src = xg_in(s, b)
-            arrival.wait_recv()
-            cg(s, b, src, False).start()
-        for s in range(n_x):
-            cg_in(s, b).wait_recv()
-        multiply(b)
-
-    for d in range(1, n_tp + 1):
-        if d < n_tp:
-
-            @pl.when(z >= d)
-            def _():
-                b = z - d
-                zg(0, b, False).wait_recv()
-
-                @pl.when(z < n_tp - 1)
-                def _():
-                    zg(0, b, False).start()
-
-                spread(b, False)
-
-            @pl.when(z + d < n_tp)
-            def _():
-                b = z + d
-                zg(1, b, False).wait_recv()
-
-                @pl.when(z > 0)
-                def _():
-                    zg(1, b, False).start()
-
-                spread(b, False)
-
-        for cond, b in sides(d - 1):
-            on(cond, functools.partial(process, b))
-
-    gate_act = acc_g[...]
-    hid[...] = (gate_act / (1.0 + jnp.exp(-gate_act)) * acc_u[...]).astype(jnp.bfloat16)
-    for s in range(1, n_ep):
-        gate_arrival(s).wait_recv()
-    experts = gall.shape[1]
-    mine = lax.broadcasted_iota(jnp.int32, (experts, 128), 0) == me
-
-    for e in range(n_ep):
-        row = jnp.sum(jnp.where(mine, gall[e], 0.0), axis=0, keepdims=True)
-        square = jnp.broadcast_to(row, (128, 128)).T
-        gcol[e * rows : (e + 1) * rows, :] = square[:rows, :]
-
-    def cr(s, b):
-        owner = x_of(s) * CORES + 1 - core
-        return remote(part.at[b, owner], from_core.at[s, b], cr_send.at[s, b], cr_recv.at[s, b], ep=other)
-
-    def xr(s, b):
-        dst = x_of(s) * CORES + core
-        return remote(part.at[b, dst], from_x.at[s - 1, b], xr_send.at[s, b], xr_recv.at[s, b], ep=dst)
-
-    down_tile = 256 if width % 256 == 0 else 128
-
-    def down(b):
-        w_copies(b)[2].wait()
-
-        def column(j, carry):
-            cols = pl.ds(pl.multiple_of(j * down_tile, down_tile), down_tile)
-            out = jnp.dot(hid[...], wd[b, :, cols], preferred_element_type=jnp.float32)
-            out = (out * gcol[:, :1]).astype(jnp.bfloat16)
-            part[b, :, :, cols] = out.reshape(n_ep, rows, down_tile)
-            return carry
-
-        lax.fori_loop(0, width // down_tile, column, 0)
-        for s in range(1, n_x):
-            cr(s, b).start()
-        cr(0, b).start()
-
-    def over_x(b):
-        for s in range(1, n_x):
-            dst = x_of(s) * CORES + core
-            cr(s, b).wait_recv()
-            part[b, dst] = (
-                part[b, dst].astype(jnp.float32) + from_core[s, b].astype(jnp.float32)
-            ).astype(jnp.bfloat16)
-            xr(s, b).start()
-
-    for d in range(n_tp - 1, -2, -1):
-        if d >= 0:
-            for cond, b in sides(d):
-                on(cond, functools.partial(down, b))
-        if d + 1 < n_tp:
-            for cond, b in sides(d + 1):
-                on(cond, functools.partial(over_x, b))
-
     def zr(direction, b):
         to = z + 1 if direction == 0 else z - 1
         return remote(
-            zsend.at[b], from_z.at[direction, b], zr_send.at[b], zr_recv.at[direction, b], tp=to
+            part.at[b, me], from_z.at[direction, b], zr_send.at[b], zr_recv.at[direction, b], tp=to
         )
 
     def chip_sum(b):
@@ -397,12 +426,12 @@
     def along(direction, b, first):
         @pl.when(first)
         def _():
-            zsend[b] = chip_sum(b).astype(jnp.bfloat16)
+            part[b, me] = chip_sum(b).astype(jnp.bfloat16)
 
         @pl.when(jnp.logical_not(first))
         def _():
             zr(direction, b).wait_recv()
-            zsend[b] = (chip_sum(b) + from_z[direction, b].astype(jnp.float32)).astype(jnp.bfloat16)
+            part[b, me] = (chip_sum(b) + from_z[direction, b].astype(jnp.float32)).astype(jnp.bfloat16)
 
         zr(direction, b).start()
 
@@ -501,20 +530,8 @@
     tokens = n_ep * rows
     experts = max(8, n_ep)
 
-    probs = jax.nn.sigmoid(router_logits)
-    gates = route_scale * probs / jnp.sum(probs, axis=1, keepdims=True)
-    names = jnp.arange(experts, dtype=jnp.int32)[:, None, None]
-    table = jnp.sum(jnp.where(routes[None] == names, gates[None], 0.0), axis=2)
-    table = jnp.pad(table, ((0, 0), (0, 128 - rows)))
-
-    q_pos = lax.axis_index("ep") * rows + jnp.arange(rows, dtype=jnp.int32)
-    k_pos = jnp.arange(tokens, dtype=jnp.int32)
-    q_prompt = prompt_of(prompt_lengths, q_pos)
-    k_prompt = prompt_of(prompt_lengths, k_pos)
-    visible = (q_prompt[:, None] == k_prompt[None, :]) & (k_pos[None, :] <= q_pos[:, None])
-    bias = jnp.where(visible, 0.0, -1.0).astype(jnp.float32)
-
     vmem = pl.BlockSpec(memory_space=pltpu.VMEM)
+    smem = pl.BlockSpec(memory_space=pltpu.SMEM)
     hbm = pl.BlockSpec(memory_space=pl.ANY)
     bf16, f32 = jnp.bfloat16, jnp.float32
     dma = pltpu.SemaphoreType.DMA
@@ -524,11 +541,14 @@
             jax.ShapeDtypeStruct((rows, width), bf16),
             jax.ShapeDtypeStruct((rows * heads, latent), bf16),
         ),
-        in_specs=[vmem] * 7 + [hbm] * 3,
+        in_specs=[vmem] * 7 + [smem] + [hbm] * 3,
         out_specs=(vmem, vmem),
         scratch_shapes=[
             pltpu.VMEM((n_tp, n_ep, rows, width), bf16),
+            pltpu.VMEM((experts, 128), f32),
             pltpu.VMEM((n_ep, experts, 128), f32),
+            pltpu.VMEM((tokens, heads * rope), bf16),
+            pltpu.VMEM((rows, tokens), f32),
             pltpu.VMEM((n_ep, rows, latent), bf16),
             pltpu.VMEM((n_ep, rows, rope), bf16),
             pltpu.VMEM((n_tp * width, units), bf16),
@@ -542,7 +562,6 @@
             pltpu.VMEM((n_x, n_tp, rows, width), bf16),
             pltpu.VMEM((n_x - 1, n_tp, rows, width), bf16),
             pltpu.VMEM((2, n_tp, rows, width), bf16),
-            pltpu.VMEM((n_tp, rows, width), bf16),
             dma((3, n_tp)),
             dma((5, n_ep)),
             dma((5, n_ep)),
@@ -565,12 +584,13 @@
         name="layer",
     )(
         x_moe,
-        table,
+        routes,
+        router_logits,
         q_latent.reshape(rows * heads, latent),
-        q_rope.reshape(rows * heads, rope),
+        q_rope,
         kv_latent,
         key_rope,
-        bias,
+        prompt_lengths,
         w_gate,
         w_up,
         w_down,

time: 79 us -> 72.7 us (0.920)
  Pallas kernels: 68.7 us -> 64.7 us
  other arithmetic: 3.13 us -> 0 us
    pallas_call x1, Pallas kernels: 68.7 us -> 64.7 us  [body(): pl.pallas_call(functools.partial(kernel, n_ep, n_tp), out_shape=(jax.Shap...]
    unnamed x2 -> x4, local copies, waits for them, and re-layouts: 3.9 us -> 6.67 us
    reshape x1 -> x0, local copies, waits for them, and re-layouts: 1.82 us -> none  [body(): q_rope.reshape(rows * heads, rope)]
    reduce_sum x4 -> x0, other arithmetic: 1.57 us -> none  [the longest x1 0.7 us: body(): table = jnp.sum(jnp.where(routes[None] == names, gates[None], 0.0), axis=2)]
    another operation x1 -> x0, other arithmetic: 0.83 us -> none
where the time goes in v2:
time: 72.7 us; the launch traced here: 72 us
  Pallas kernels  64.7 us (89%)
  local copies, waits for them, and re-layouts  6.67 us (9%)
    pallas_call x1, Pallas kernels, body(): pl.pallas_call(functools.partial(kernel, n_ep, n_tp), out_shape=(jax.Shap...  64.7 us
    unnamed x4, local copies, waits for them, and re-layouts  6.67 us

profile of v2, /device:TPU:0, one launch (start us, length us, event | category | flops | bytes accessed | tf_op | source)
XLA Modules:
  0.0 72.0 jit_solution(17227116224672656930)
XLA Ops:
  0.6 1.4 %copy.13.routes_ref = s32[64,2]{1,0:T(8,128)} copy(s32[64,2]{0,1:T(2,128)} %param.12) | data formatting | bytes 1024 | tf_op args[1]
  2.0 1.4 %copy.14.logits_ref = f32[64,2]{1,0:T(8,128)} copy(f32[64,2]{0,1:T(2,128)} %param.13) | data formatting | bytes 1024 | tf_op args[2]
  3.4 64.7 %layer.1 = (bf16[64,1792]{1,0:T(8,128)(2,1)}, bf16[1024,512]{1,0:T(8,128)(2,1)}) custom-call(bf16[64,1792]{1,0:T(8,128)(2,1)} %x_ref.1, s32[64,2]{1,0:T(8,128)} %copy.13.routes_ref, f32[64,2]{1,0:T(8,128)} %copy.14.logits_ref, bf16[1024,512]{1,0:T(8,128)(2,1)} %bitcast.2, bf16[64,1024]{1,0:T(8,128)(2,1)} %qr_ref.1, bf16[64,512]{1,0:T(8,128)(2,1)} %kv_ref.1, ...), custom_call_target="tpu_custom_call" | custom-call | tf_op jit(solution)/shard_map/layer/pallas_call | solution.py:538
  68.1 1.6 %copy.17 = bf16[64,1792]{1,0:T(8,128)(2,1)} copy(bf16[64,1792]{1,0:T(8,128)(2,1)} %get-tuple-element.8) | data formatting | bytes 458752
  69.8 2.3 %copy.18 = bf16[64,16,512]{2,1,0:T(8,128)(2,1)} copy(bf16[64,16,512]{2,1,0:T(8,128)(2,1)} %bitcast.3) | data formatting | bytes 2097152

commit v3 on v2

--- a/solution.py
+++ b/solution.py
@@ -132,13 +132,13 @@
         pl.semaphore_signal(barrier, inc=1, device_id={"tp": z + 1}, device_id_type=MESH)
 
     probs = 1.0 / (1.0 + jnp.exp(-logits_ref[...]))
-    gates = route_scale * probs / jnp.sum(probs, axis=1, keepdims=True)
-    lanes = lax.broadcasted_iota(jnp.int32, (rows, 128), 1)
-    table = jnp.zeros((rows, 128), jnp.float32)
-    for k in range(routes_ref.shape[1]):
-        table += jnp.where(routes_ref[:, k : k + 1] == lanes, gates[:, k : k + 1], 0.0)
-    square = jnp.concatenate([table, jnp.zeros((128 - rows, 128), jnp.float32)], axis=0)
-    gt_ref[...] = square.T[: gt_ref.shape[0], :]
+    gates = route_scale * probs / jnp.sum(probs, axis=0, keepdims=True)
+    names = lax.broadcasted_iota(jnp.int32, (gt_ref.shape[0], rows), 0)
+    table = jnp.zeros((gt_ref.shape[0], rows), jnp.float32)
+    for k in range(routes_ref.shape[0]):
+        table += jnp.where(routes_ref[k : k + 1, :] == names, gates[k : k + 1, :], 0.0)
+    gt_ref[...] = jnp.zeros_like(gt_ref)
+    gt_ref[:, :rows] = table
 
     edge = (z == 0) | (z == n_tp - 1)
 
@@ -584,8 +584,8 @@
         name="layer",
     )(
         x_moe,
-        routes,
-        router_logits,
+        routes.T,
+        router_logits.T,
         q_latent.reshape(rows * heads, latent),
         q_rope,
         kv_latent,

time: 72.7 us -> 69.9 us (0.961)
  local copies, waits for them, and re-layouts: 6.67 us -> 3.9 us
    unnamed x4 -> x2, local copies, waits for them, and re-layouts: 6.67 us -> 3.9 us
where the time goes in v3:
time: 69.9 us; the launch traced here: 69.3 us
  Pallas kernels  64.8 us (93%)
  local copies, waits for them, and re-layouts  3.9 us (6%)
    pallas_call x1, Pallas kernels, body(): pl.pallas_call(functools.partial(kernel, n_ep, n_tp), out_shape=(jax.Shap...  64.8 us
    unnamed x2, local copies, waits for them, and re-layouts  3.9 us

profile of v3, /device:TPU:0, one launch (start us, length us, event | category | flops | bytes accessed | tf_op | source)
XLA Modules:
  0.0 69.3 jit_solution(13300979882377572464)
XLA Ops:
  0.6 64.8 %layer.1 = (bf16[64,1792]{1,0:T(8,128)(2,1)}, bf16[1024,512]{1,0:T(8,128)(2,1)}) custom-call(bf16[64,1792]{1,0:T(8,128)(2,1)} %x_ref.1, s32[2,64]{1,0:T(2,128)} %bitcast.6, f32[2,64]{1,0:T(2,128)} %bitcast.7, bf16[1024,512]{1,0:T(8,128)(2,1)} %bitcast.4, bf16[64,1024]{1,0:T(8,128)(2,1)} %qr_ref.1, bf16[64,512]{1,0:T(8,128)(2,1)} %kv_ref.1, ...), custom_call_target="tpu_custom_call" | custom-call | tf_op jit(solution)/shard_map/layer/pallas_call | solution.py:538
  65.4 1.6 %copy.15 = bf16[64,1792]{1,0:T(8,128)(2,1)} copy(bf16[64,1792]{1,0:T(8,128)(2,1)} %get-tuple-element.8) | data formatting | bytes 458752
  67.0 2.3 %copy.16 = bf16[64,16,512]{2,1,0:T(8,128)(2,1)} copy(bf16[64,16,512]{2,1,0:T(8,128)(2,1)} %bitcast.5) | data formatting | bytes 2097152
